TPU v7x, 256 devices: a whole 4x4x8 slice. The times are simulated.
256 devices in a mesh: mem: 4 (over z_hi), lat: 64 (over x, z_lo, y, core).
Axes of the slice: x: 4, y: 4, z: 8 (z_hi: 4, z_lo: 2; z = z_hi * 2 + z_lo), core: 2. Of those that a mesh axis runs over, the one named last changes fastest.
Arguments:
- members: float32 [32, 2, 512, 1024], P('mem', None, 'lat'), may hold values from -0.75 to 0.75
- lat_root: float32 [512, 512], replicated, may hold values from -1 to 2
- lon_root: float32 [1024, 1024], replicated, may hold values from -1 to 2
- innovation: float32 [512, 256], P('lat', 'mem'), may hold values from -6 to 6
- obs_weight: float32 [512, 256], P('lat', 'mem'), may hold values from 0.5 to 4
- obs_mask: int32 [512, 256], P('lat', 'mem'), may hold values 0 or 1
- obs_cell: int32 [512, 256], P('lat', 'mem'), may hold values from 0 to 2047, as said below
Outputs:
- increment: float32 [2, 512, 1024], P(None, 'lat', 'mem')
- control: float32 [32, 2, 512, 1024], P('mem', None, 'lat')
Inputs may be any that keep to these rules, and one draw needn't show every extreme that they name: `obs_cell`: entry e in column c has (e % 1024) // 256 equal to c // 64.
All inputs are finite; a program needn't handle non-finite values. No bound on the sum of `obs_mask` on one device may be relied on, other than what follows from the above.
Results may differ from a plain program's by a relative error of at most 0.0003.
Values sent between devices are 32-bit elements; how exact they have to be, the bound alone decides.
A program may use at most 64 MiB of HBM per device.

v0:
```python
import jax
import jax.numpy as jnp
from jax import lax
from jax.sharding import Mesh
from jax.sharding import PartitionSpec as P

LON_BLOCK = 128
INNER = 2
LAT = ("lat_0", "lat_1", "lat_2", "lat_3")
MEM_LAT = ("mem", "lat_0", "lat_1", "lat_2", "lat_3")
HIGH = lax.Precision.HIGHEST


def in_blocks(shard, dim, count):
    dims = shard.shape
    tiles = shard.reshape(*dims[:dim], count, dims[dim] // count, *dims[dim + 1 :])
    return jnp.moveaxis(tiles, dim, 0)


def summed_on_arrival(shard, axis, dim):
    tiles = in_blocks(shard, dim, lax.axis_size(axis))
    arrived = lax.all_to_all(tiles, axis, split_axis=0, concat_axis=0, tiled=True)
    return arrived.sum(axis=0)


def joined_along(tiles, dim):
    tiles = jnp.moveaxis(tiles, 0, dim)
    dims = tiles.shape
    return tiles.reshape(*dims[:dim], dims[dim] * dims[dim + 1], *dims[dim + 2 :])


def from_everyone(shard, axis):
    count = lax.axis_size(axis)
    return lax.all_to_all(
        jnp.broadcast_to(shard[None], (count, *shard.shape)), axis, 0, 0, tiled=True
    )


def gathered_copies(shard, axis, dim):
    return joined_along(from_everyone(shard, axis), dim)


def by_axis(shard, axes):
    for axis in axes:
        shard = lax.psum(shard, axis)
    return shard


def per_device(members, lat_root, lon_root, innovation, obs_weight, obs_mask, obs_cell):
    mem_dev, levels, rows, nlon = members.shape
    nblocks = nlon // LON_BLOCK
    fields = mem_dev * levels
    quarter = nlon // lax.axis_size("mem")
    lon_pair = lon_root.reshape(nlon, nblocks, LON_BLOCK)
    weights = obs_weight * obs_mask.astype(jnp.float32)
    local_cell = obs_cell // nlon * quarter + obs_cell % nlon - lax.axis_index("mem") * quarter
    row_ids = jnp.broadcast_to(jnp.arange(rows, dtype=jnp.int32)[:, None], obs_cell.shape)

    def to_strips(blocked):
        return lax.all_to_all(blocked, LAT, split_axis=0, concat_axis=1, tiled=True)

    def to_rows(strips):
        return lax.all_to_all(strips, LAT, split_axis=1, concat_axis=0, tiled=True)

    def latitude(strips, adjoint):
        form = "ji,pjc->pic" if adjoint else "ij,pjc->pic"
        return jnp.einsum(form, lat_root, strips, precision=HIGH)

    def lon_adjoint(field):
        blocked = jnp.einsum("frn,nbc->fbrc", field, lon_pair, precision=HIGH)
        return blocked.reshape(fields * nblocks, rows, LON_BLOCK)

    def adjoint(field):
        return latitude(to_strips(lon_adjoint(field)), True)

    def spread(values):
        flat = jnp.zeros((rows, levels * quarter), jnp.float32).at[row_ids, local_cell].add(values)
        field = flat.reshape(rows, levels, quarter).transpose(1, 0, 2)
        whole = gathered_copies(field, "mem", 2)
        return adjoint((members * whole[None]).reshape(fields, rows, nlon))

    def squares(vector):
        return by_axis(jnp.sum(vector * vector), MEM_LAT)

    gradient = spread(-(weights * innovation))
    control = jnp.zeros_like(gradient)
    increment = jnp.zeros((levels, rows, quarter), jnp.float32)
    norm_now = squares(gradient)
    for step in range(INNER):
        lon_shaped = to_rows(latitude(gradient, False)).reshape(fields, nblocks, rows, LON_BLOCK)
        partial_value = jnp.sum(
            members
            * jnp.einsum("fbrc,nbc->frn", lon_shaped, lon_pair, precision=HIGH).reshape(
                mem_dev, levels, rows, nlon
            ),
            axis=0,
        )
        image = summed_on_arrival(partial_value, "mem", 2)
        observe_flat = image.transpose(1, 0, 2).reshape(rows, levels * quarter)
        curved = gradient + spread(weights * jnp.take_along_axis(observe_flat, local_cell, axis=1))
        length = norm_now / by_axis(jnp.sum(gradient * curved), MEM_LAT)
        control = control - length * gradient
        increment = increment - length * image
        gradient = gradient - length * curved
        if step + 1 < INNER:
            norm_now = squares(gradient)
    shaped = to_rows(control).reshape(fields, nblocks, rows, LON_BLOCK).transpose(0, 2, 1, 3)
    control = shaped.reshape(fields, rows, nlon)
    return (increment, control.reshape(mem_dev, levels, rows, nlon))


def solution(mesh):
    finer = Mesh(
        mesh.devices.reshape(mesh.shape["mem"], 4, 2, 4, 2),
        ("mem", "lat_0", "lat_1", "lat_2", "lat_3"),
    )
    placed = (
        P("mem", None, LAT, None),
        P(),
        P(),
        P(LAT, "mem"),
        P(LAT, "mem"),
        P(LAT, "mem"),
        P(LAT, "mem"),
    )
    return jax.shard_map(
        per_device,
        mesh=finer,
        in_specs=placed,
        out_specs=(P(None, LAT, "mem"), P("mem", None, LAT, None)),
        check_vma=False,
    )
```

profile of v0, /device:TPU:1, one launch (start us, length us, event | category | flops | bytes accessed | tf_op | source)
XLA Modules:
  0.0 367.9 jit_solution(17815400289269395363)
XLA Ops:
  0.6 0.0 copy-start
  0.6 0.8 fusion.46
  1.5 0.1 reshape.118
  1.5 0.7 multiply_negate_fusion
  2.3 0.1 reshape.120
  2.3 23.9 %scatter_fusion = f32[8,512]{1,0:T(8,128)S(1)} fusion(f32[8,512]{1,0:T(8,128)S(1)} %broadcast.43.clone, s32[512]{0:T(512)S(1)} %reshape.118, f32[512]{0:T(512)S(1)} %reshape.120), kind=kCustom, calls=%fused_computation.2 | custom fusion | flops 512 | bytes 10240 | tf_op jit(solution)/shard_map/scatter-add | solution.py:77
  26.3 15.9 %all_to_all.124 = f32[4,2,8,256]{3,2,1,0:T(8,128)S(1)} all-to-all(f32[4,2,8,256]{3,2,1,0:T(8,128)S(1)} %broadcast_in_dim.20), channel_id=1, replica_groups=mesh['mem'=4,'lat_0'=4,'lat_1'=2,'lat_2'=4,'lat_3'=2] {'mem'}, dimensions={0} | all-to-all | bytes 131072 | tf_op jit(solution)/shard_map/all_to_all | solution.py:34
  42.1 0.0 copy-done.1
  42.2 4.6 %fusion.2 = f32[16,8,8,128]{3,1,2,0:T(8,128)S(1)} fusion(f32[16,8,1024,1]{2,1,3,0:T(8,128)S(1)} %bitcast.204, f32[1024,1024]{1,0:T(8,128)} %param.11), kind=kOutput, calls=%fused_computation.8 | convolution fusion | flops 1610612736 | bytes 5242880 | tf_op jit(solution)/shard_map/frn,nbc->fbrc/dot_general | solution.py:70
  46.8 22.3 %all_to_all.125 = f32[128,8,128]{2,1,0:T(8,128)S(1)} all-to-all(f32[128,8,128]{2,1,0:T(8,128)S(1)} %bitcast.205), channel_id=1, replica_groups=mesh['mem'=4,'lat_0'=4,'lat_1'=2,'lat_2'=4,'lat_3'=2] {'lat_0','lat_1','..., dimensions={0} | all-to-all | bytes 1048576 | tf_op jit(solution)/shard_map/all_to_all | solution.py:60
  69.1 0.0 copy-done
  69.1 1.1 convolution_bitcast_fusion.4
  70.2 1.1 convolution_bitcast_fusion.3
  71.2 1.0 copy.72
  72.2 4.6 %all-to-all-start.2 = ((f32[2,512,128]{2,0,1:T(2,128)}), f32[2,512,128]{2,0,1:T(2,128)S(1)}, u32[]{:S(2)}, u32[]{:S(2)}) async-start(f32[2,512,128]{2,0,1:T(2,128)} %copy.72), calls=%async_computation.2 | async-start | bytes 1048576 | tf_op jit(solution)/shard_map/all_to_all | solution.py:63
  76.9 5.1 %copy.111 = f32[128,8,8,128]{3,2,1,0:T(8,128)} copy(f32[128,8,8,128]{3,1,2,0:T(8,128)} %bitcast.200) | data formatting | bytes 8388608
  82.0 7.3 %all-to-all-done.2 = f32[2,512,128]{2,0,1:T(2,128)S(1)} async-done(((f32[2,512,128]{2,0,1:T(2,128)}), f32[2,512,128]{2,0,1:T(2,128)S(1)}, u32[]{:S(2)}, u32[]{:S(2)}) %all-to-all-start.2) | async-done | bytes 524320 | tf_op jit(solution)/shard_map/all_to_all | solution.py:63
  89.4 6.8 %fusion.25 = f32[2,8,1024]{2,1,0:T(8,128)S(1)} fusion(f32[8,2,8,1024]{3,2,1,0:T(8,128)S(1)} %copy-done.1, f32[8,2,8,8,128]{4,2,3,1,0:T(8,128)S(1)} %bitcast.217, f32[1024,8,128,1,1]{2,1,0,4,3:T(8,128)} %bitcast.201), kind=kOutput, calls=%fused_computation.28 | convolution fusion | flops 1610858496 | bytes 5308416 | tf_op jit(solution)/shard_map/fbrc,nbc->frn/dot_general | solution.py:93
  96.3 0.0 copy-start.2
  96.3 0.0 copy-start.3
  96.3 0.6 copy.76
  97.0 3.3 all-to-all-start.3
  100.3 0.1 reshape.147
  100.3 6.8 %all-to-all-done.3 = f32[4,2,8,256]{3,2,1,0:T(8,128)S(1)} async-done(((f32[4,2,8,256]{3,2,1,0:T(8,128)}), f32[4,2,8,256]{3,2,1,0:T(8,128)S(1)}, u32[]{:S(2)}, u32[]{:S(2)}) %all-to-all-start.3) | async-done | bytes 65568 | tf_op jit(solution)/shard_map/all_to_all | solution.py:22
  107.1 3.6 gather_fusion
  110.7 0.1 reshape.150
  110.8 0.0 copy-done.2
  110.8 0.0 copy-done.3
  110.8 0.1 reshape.126
  110.9 23.9 %scatter_fusion.1 = f32[8,512]{1,0:T(8,128)S(1)} fusion(f32[8,512]{1,0:T(8,128)S(1)} %broadcast.43.clone.1, s32[512]{0:T(512)S(1)} %reshape.118, f32[512]{0:T(512)S(1)} %reshape.126), kind=kCustom, calls=%fused_computation.3 | custom fusion | flops 512 | bytes 10240 | tf_op jit(solution)/shard_map/scatter-add | solution.py:77
  134.8 9.3 %all_to_all.126 = f32[4,2,8,256]{3,2,1,0:T(8,128)S(1)} all-to-all(f32[4,2,8,256]{3,2,1,0:T(8,128)S(1)} %broadcast_in_dim.21), channel_id=1, replica_groups=mesh['mem'=4,'lat_0'=4,'lat_1'=2,'lat_2'=4,'lat_3'=2] {'mem'}, dimensions={0} | all-to-all | bytes 131072 | tf_op jit(solution)/shard_map/all_to_all | solution.py:34
  144.2 4.6 %fusion.1 = f32[16,8,8,128]{3,1,2,0:T(8,128)S(1)} fusion(f32[16,8,1024,1]{2,1,3,0:T(8,128)S(1)} %bitcast.206, f32[1024,1024]{1,0:T(8,128)} %param.11), kind=kOutput, calls=%fused_computation.7 | convolution fusion | flops 1610612736 | bytes 5242880 | tf_op jit(solution)/shard_map/frn,nbc->fbrc/dot_general | solution.py:70
  148.8 19.5 %all_to_all.127 = f32[128,8,128]{2,1,0:T(8,128)S(1)} all-to-all(f32[128,8,128]{2,1,0:T(8,128)S(1)} %bitcast.207), channel_id=1, replica_groups=mesh['mem'=4,'lat_0'=4,'lat_1'=2,'lat_2'=4,'lat_3'=2] {'lat_0','lat_1','..., dimensions={0} | all-to-all | bytes 1048576 | tf_op jit(solution)/shard_map/all_to_all | solution.py:60
  168.3 1.8 multiply_reduce_fusion.1
  170.1 7.8 %all-reduce.5 = (f32[]{:T(128)}, f32[]{:T(128)}) all-reduce(f32[]{:T(128)} %get-tuple-element.4, f32[]{:T(128)} %get-tuple-element.3), channel_id=1, replica_groups=mesh['mem'=4,'lat_0'=4,'lat_1'=2,'lat_2'=4,'lat_3'=2] {'mem'}, use_global_device_ids=true, to_apply=%region_2.3 | all-reduce | flops 2 | bytes 16 | tf_op jit(solution)/shard_map/psum | solution.py:45
  177.9 7.4 %all-reduce.3 = (f32[]{:T(128)}, f32[]{:T(128)}) all-reduce(f32[]{:T(128)} %get-tuple-element.15, f32[]{:T(128)} %get-tuple-element.16), channel_id=1, replica_groups=mesh['mem'=4,'lat_0'=4,'lat_1'=2,'lat_2'=4,'lat_3'=2] {'lat_0'}, use_global_device_ids=true, to_apply=%region_3.4 | all-reduce | flops 2 | bytes 16 | tf_op jit(solution)/shard_map/psum | solution.py:45
  185.3 4.4 %all-reduce.9 = (f32[]{:T(128)}, f32[]{:T(128)}) all-reduce(f32[]{:T(128)} %get-tuple-element.11, f32[]{:T(128)} %get-tuple-element.12), channel_id=1, replica_groups=mesh['mem'=4,'lat_0'=4,'lat_1'=2,'lat_2'=4,'lat_3'=2] {'lat_1'}, use_global_device_ids=true, to_apply=%region_4.5 | all-reduce | flops 2 | bytes 16 | tf_op jit(solution)/shard_map/psum | solution.py:45
  189.7 7.1 %all-reduce.1 = (f32[]{:T(128)}, f32[]{:T(128)}) all-reduce(f32[]{:T(128)} %get-tuple-element.23, f32[]{:T(128)} %get-tuple-element.24), channel_id=1, replica_groups=mesh['mem'=4,'lat_0'=4,'lat_1'=2,'lat_2'=4,'lat_3'=2] {'lat_2'}, use_global_device_ids=true, to_apply=%region_5.6 | all-reduce | flops 2 | bytes 16 | tf_op jit(solution)/shard_map/psum | solution.py:45
  196.7 10.6 %all-reduce.7 = (f32[]{:T(128)}, f32[]{:T(128)}) all-reduce(f32[]{:T(128)} %get-tuple-element.7, f32[]{:T(128)} %get-tuple-element.8), channel_id=1, replica_groups=mesh['mem'=4,'lat_0'=4,'lat_1'=2,'lat_2'=4,'lat_3'=2] {'lat_3'}, use_global_device_ids=true, to_apply=%region_6.7 | all-reduce | flops 2 | bytes 16 | tf_op jit(solution)/shard_map/psum | solution.py:45
  208.7 0.8 multiply_reduce_fusion
  209.5 1.9 convolution_bitcast_fusion.1
  211.3 1.3 copy.81
  212.6 16.5 %all_to_all.128 = f32[2,512,128]{2,0,1:T(2,128)S(1)} all-to-all(f32[2,512,128]{2,0,1:T(2,128)S(1)} %copy.81), channel_id=1, replica_groups=mesh['mem'=4,'lat_0'=4,'lat_1'=2,'lat_2'=4,'lat_3'=2] {'lat_0','lat_1','..., dimensions={1} | all-to-all | bytes 1048576 | tf_op jit(solution)/shard_map/all_to_all | solution.py:63
  229.2 6.8 %fusion.28 = f32[2,8,1024]{2,1,0:T(8,128)S(1)} fusion(f32[8,2,8,1024]{3,2,1,0:T(8,128)S(1)} %copy-done.1, f32[8,2,8,8,128]{4,2,3,1,0:T(8,128)S(1)} %bitcast.216, f32[1024,8,128,1,1]{2,1,0,4,3:T(8,128)} %bitcast.202), kind=kOutput, calls=%fused_computation.29 | convolution fusion | flops 1610858496 | bytes 5308416 | tf_op jit(solution)/shard_map/fbrc,nbc->frn/dot_general | solution.py:93
  236.1 11.6 %all_to_all.131 = f32[4,2,8,256]{3,2,1,0:T(8,128)S(1)} all-to-all(f32[4,2,8,256]{3,2,1,0:T(8,128)S(1)} %copy.85), channel_id=1, replica_groups=mesh['mem'=4,'lat_0'=4,'lat_1'=2,'lat_2'=4,'lat_3'=2] {'mem'}, dimensions={0} | all-to-all | bytes 131072 | tf_op jit(solution)/shard_map/all_to_all | solution.py:22
  247.7 3.6 gather_fusion.1
  251.3 0.1 reshape.155
  251.4 0.1 reshape.132
  251.5 23.9 %scatter_fusion.2 = f32[8,512]{1,0:T(8,128)S(1)} fusion(f32[8,512]{1,0:T(8,128)S(1)} %broadcast.43, s32[512]{0:T(512)S(1)} %reshape.118, f32[512]{0:T(512)S(1)} %reshape.132), kind=kCustom, calls=%fused_computation.4 | custom fusion | flops 512 | bytes 10240 | tf_op jit(solution)/shard_map/scatter-add | solution.py:77
  275.4 9.3 %all_to_all.129 = f32[4,2,8,256]{3,2,1,0:T(8,128)S(1)} all-to-all(f32[4,2,8,256]{3,2,1,0:T(8,128)S(1)} %broadcast_in_dim.22), channel_id=1, replica_groups=mesh['mem'=4,'lat_0'=4,'lat_1'=2,'lat_2'=4,'lat_3'=2] {'mem'}, dimensions={0} | all-to-all | bytes 131072 | tf_op jit(solution)/shard_map/all_to_all | solution.py:34
  284.7 4.6 %fusion = f32[16,8,8,128]{3,1,2,0:T(8,128)S(1)} fusion(f32[16,8,1024,1]{2,1,3,0:T(8,128)S(1)} %bitcast.208, f32[1024,1024]{1,0:T(8,128)} %param.11), kind=kOutput, calls=%fused_computation.6 | convolution fusion | flops 1610612736 | bytes 5242880 | tf_op jit(solution)/shard_map/frn,nbc->fbrc/dot_general | solution.py:70
  289.3 19.5 %all_to_all.130 = f32[128,8,128]{2,1,0:T(8,128)S(1)} all-to-all(f32[128,8,128]{2,1,0:T(8,128)S(1)} %bitcast.209), channel_id=1, replica_groups=mesh['mem'=4,'lat_0'=4,'lat_1'=2,'lat_2'=4,'lat_3'=2] {'lat_0','lat_1','..., dimensions={0} | all-to-all | bytes 1048576 | tf_op jit(solution)/shard_map/all_to_all | solution.py:60
  308.8 1.7 fusion.36
  310.5 7.8 %all-reduce.4 = (f32[]{:T(128)}, f32[]{:T(128)}) all-reduce(f32[]{:T(128)} %get-tuple-element.25, f32[]{:T(128)} %fusion.36), channel_id=1, replica_groups=mesh['mem'=4,'lat_0'=4,'lat_1'=2,'lat_2'=4,'lat_3'=2] {'mem'}, use_global_device_ids=true, to_apply=%region_17.19 | all-reduce | flops 2 | bytes 16 | tf_op jit(solution)/shard_map/psum | solution.py:45
  318.3 7.4 %all-reduce.2 = (f32[]{:T(128)}, f32[]{:T(128)}) all-reduce(f32[]{:T(128)} %get-tuple-element.13, f32[]{:T(128)} %get-tuple-element.14), channel_id=1, replica_groups=mesh['mem'=4,'lat_0'=4,'lat_1'=2,'lat_2'=4,'lat_3'=2] {'lat_0'}, use_global_device_ids=true, to_apply=%region_18.20 | all-reduce | flops 2 | bytes 16 | tf_op jit(solution)/shard_map/psum | solution.py:45
  325.7 4.4 %all-reduce.8 = (f32[]{:T(128)}, f32[]{:T(128)}) all-reduce(f32[]{:T(128)} %get-tuple-element.9, f32[]{:T(128)} %get-tuple-element.10), channel_id=1, replica_groups=mesh['mem'=4,'lat_0'=4,'lat_1'=2,'lat_2'=4,'lat_3'=2] {'lat_1'}, use_global_device_ids=true, to_apply=%region_19.21 | all-reduce | flops 2 | bytes 16 | tf_op jit(solution)/shard_map/psum | solution.py:45
  330.1 7.1 %all-reduce = (f32[]{:T(128)}, f32[]{:T(128)}) all-reduce(f32[]{:T(128)} %get-tuple-element.21, f32[]{:T(128)} %get-tuple-element.22), channel_id=1, replica_groups=mesh['mem'=4,'lat_0'=4,'lat_1'=2,'lat_2'=4,'lat_3'=2] {'lat_2'}, use_global_device_ids=true, to_apply=%region_20.22 | all-reduce | flops 2 | bytes 16 | tf_op jit(solution)/shard_map/psum | solution.py:45
  337.2 10.4 %all-reduce.6 = (f32[]{:T(128)}, f32[]{:T(128)}) all-reduce(f32[]{:T(128)} %get-tuple-element.5, f32[]{:T(128)} %get-tuple-element.6), channel_id=1, replica_groups=mesh['mem'=4,'lat_0'=4,'lat_1'=2,'lat_2'=4,'lat_3'=2] {'lat_3'}, use_global_device_ids=true, to_apply=%region_21.23 | all-reduce | flops 2 | bytes 16 | tf_op jit(solution)/shard_map/psum | solution.py:45
  348.9 0.1 multiply_subtract_fusion
  349.0 1.0 copy.90
  350.0 4.4 %all-to-all-start.10 = ((f32[2,512,128]{2,0,1:T(2,128)}), f32[2,512,128]{2,0,1:T(2,128)S(1)}, u32[]{:S(2)}, u32[]{:S(2)}) async-start(f32[2,512,128]{2,0,1:T(2,128)} %copy.90), calls=%async_computation.10 | async-start | bytes 1048576 | tf_op jit(solution)/shard_map/all_to_all | solution.py:63
  354.4 0.6 multiply_subtract_fusion.2
  355.1 11.9 %all-to-all-done.10 = f32[2,512,128]{2,0,1:T(2,128)S(1)} async-done(((f32[2,512,128]{2,0,1:T(2,128)}), f32[2,512,128]{2,0,1:T(2,128)S(1)}, u32[]{:S(2)}, u32[]{:S(2)}) %all-to-all-start.10) | async-done | bytes 524320 | tf_op jit(solution)/shard_map/all_to_all | solution.py:63
  367.0 0.8 copy.92
  (26 shorter events, 0.5 us)
Async XLA Ops:
  0.6 68.5 %copy-start = (f32[512,512]{1,0:T(8,128)S(1)}, f32[512,512]{1,0:T(8,128)}, u32[]{:S(2)}) copy-start(f32[512,512]{1,0:T(8,128)} %param.10) | copy-start | bytes 3145732
  2.3 39.8 %copy-start.1 = (f32[8,2,8,1024]{3,2,1,0:T(8,128)S(1)}, f32[8,2,8,1024]{3,2,1,0:T(8,128)}, u32[]{:S(2)}) copy-start(f32[8,2,8,1024]{3,2,1,0:T(8,128)} %param.9) | copy-start | bytes 1572868
  72.2 17.1 %all-to-all-start.2 = ((f32[2,512,128]{2,0,1:T(2,128)}), f32[2,512,128]{2,0,1:T(2,128)S(1)}, u32[]{:S(2)}, u32[]{:S(2)}) async-start(f32[2,512,128]{2,0,1:T(2,128)} %copy.72), calls=%async_computation.2 | async-start | bytes 1048576 | tf_op jit(solution)/shard_map/all_to_all | solution.py:63
  96.3 14.5 %copy-start.2 = (f32[8,64]{1,0:T(8,128)S(1)}, f32[8,64]{1,0:T(8,128)}, u32[]{:S(2)}) copy-start(f32[8,64]{1,0:T(8,128)} %param.13) | copy-start | bytes 6148
  96.3 14.5 %copy-start.3 = (s32[8,64]{1,0:T(8,128)S(1)}, s32[8,64]{1,0:T(8,128)}, u32[]{:S(2)}) copy-start(s32[8,64]{1,0:T(8,128)} %param.14) | copy-start | bytes 6148
  97.0 10.1 %all-to-all-start.3 = ((f32[4,2,8,256]{3,2,1,0:T(8,128)}), f32[4,2,8,256]{3,2,1,0:T(8,128)S(1)}, u32[]{:S(2)}, u32[]{:S(2)}) async-start(f32[4,2,8,256]{3,2,1,0:T(8,128)} %copy.76), calls=%async_computation.3 | async-start | bytes 131072 | tf_op jit(solution)/shard_map/all_to_all | solution.py:22
  350.0 17.0 %all-to-all-start.10 = ((f32[2,512,128]{2,0,1:T(2,128)}), f32[2,512,128]{2,0,1:T(2,128)S(1)}, u32[]{:S(2)}, u32[]{:S(2)}) async-start(f32[2,512,128]{2,0,1:T(2,128)} %copy.90), calls=%async_computation.10 | async-start | bytes 1048576 | tf_op jit(solution)/shard_map/all_to_all | solution.py:63
where the time goes:
time: 369 us; the launch traced here: 368 us
  blocking collectives  198 us (54%)
  other arithmetic  74.9 us (20%)
  matrix products  35 us (9%)
  waiting for transfers between devices  26.1 us (7%)
  local copies, waits for them, and re-layouts  17.9 us (5%)
  starting transfers between devices  12.3 us (3%)
    psum x10, blocking collectives, by_axis(): shard = lax.psum(shard, axis)  74.3 us
    scatter-add x3, other arithmetic, spread(): jnp.zeros((rows, levels * quarter), jnp.float32).at[row_ids, local_cell]  71.8 us
    all_to_all x3, blocking collectives, to_strips(): return lax.all_to_all(blocked, LAT, split_axis=0, concat_axis=1, tiled=True)  61.3 us
    all_to_all x3, blocking collectives, from_everyone(): lax.all_to_all(jnp.broadcast_to(shard[None], (count, *shard.shape)), axis...  34.4 us
    all_to_all x2, waiting for transfers between devices, to_rows(): return lax.all_to_all(strips, LAT, split_axis=1, concat_axis=0, tiled=True)  19.3 us
    all_to_all x1, blocking collectives, to_rows(): return lax.all_to_all(strips, LAT, split_axis=1, concat_axis=0, tiled=True)  16.5 us
    dot_general x3, matrix products, lon_adjoint(): blocked = jnp.einsum('frn,nbc->fbrc', field, lon_pair, precision=HIGH)  13.8 us
    dot_general x2, matrix products, per_device(): jnp.einsum('fbrc,nbc->frn', lon_shaped, lon_pair, precision=HIGH)  13.7 us
  transfers between devices with their start and end apart: 3, of which 3 were waited for; matrix products, arithmetic and copies ran while one was open for 2% of the time, Pallas kernels for 0%

commit v1 on v0

--- a/solution.py
+++ b/solution.py
@@ -42,7 +42,7 @@
 
 def by_axis(shard, axes):
     for axis in axes:
-        shard = lax.psum(shard, axis)
+        shard = jnp.sum(lax.all_gather(shard, axis), axis=0)
     return shard
 
 

time: 369 us -> 412 us (1.12); the launches traced: 368 us -> 405 us
  blocking collectives: 198 us -> 153 us
  local copies, waits for them, and re-layouts: 17.9 us -> 48.5 us
  waiting for transfers between devices: 26.1 us -> 48.7 us
  starting transfers between devices: 12.3 us -> 27.4 us
  other arithmetic: 74.9 us -> 87 us
    psum x10 -> x0, blocking collectives: 74.3 us -> none  [by_axis(): shard = lax.psum(shard, axis)]
    unnamed x0 -> x10, blocking collectives: none -> 67.8 us
    all_to_all x3 -> x1, blocking collectives: 61.3 us -> 22.3 us  [to_strips(): return lax.all_to_all(blocked, LAT, split_axis=0, concat_axis=1, tiled=True)]
    unnamed x9 -> x64, local copies, waits for them, and re-layouts: 5.15 us -> 35.8 us
    all_to_all x0 -> x2, waiting for transfers between devices: none -> 22.7 us  [to_strips(): return lax.all_to_all(blocked, LAT, split_axis=0, concat_axis=1, tiled=True)]
    all_to_all x0 -> x2, starting transfers between devices: none -> 14.5 us  [to_strips(): return lax.all_to_all(blocked, LAT, split_axis=0, concat_axis=1, tiled=True)]
    reduce_sum x0 -> x20, other arithmetic: none -> 12 us  [by_axis(): shard = jnp.sum(lax.all_gather(shard, axis), axis=0)]
  transfers between devices with their start and end apart: 3 -> 5, of which waited for: 3 -> 5; matrix products, arithmetic and copies ran while one was open for 2% -> 2% of each run, Pallas kernels for 0% -> 0%
where the time goes in v1:
time: 412 us; the launch traced here: 405 us
  blocking collectives  153 us (37%)
  other arithmetic  87 us (21%)
  waiting for transfers between devices  48.7 us (12%)
  local copies, waits for them, and re-layouts  48.5 us (12%)
  matrix products  36.6 us (9%)
  starting transfers between devices  27.4 us (7%)
    scatter-add x3, other arithmetic, spread(): jnp.zeros((rows, levels * quarter), jnp.float32).at[row_ids, local_cell]  71.8 us
    unnamed x10, blocking collectives  67.8 us
    unnamed x64, local copies, waits for them, and re-layouts  35.8 us
    all_to_all x3, blocking collectives, from_everyone(): lax.all_to_all(jnp.broadcast_to(shard[None], (count, *shard.shape)), axis...  34.4 us
    all_to_all x2, waiting for transfers between devices, to_strips(): return lax.all_to_all(blocked, LAT, split_axis=0, concat_axis=1, tiled=True)  22.7 us
    all_to_all x1, blocking collectives, to_strips(): return lax.all_to_all(blocked, LAT, split_axis=0, concat_axis=1, tiled=True)  22.3 us
    all_to_all x2, waiting for transfers between devices, to_rows(): return lax.all_to_all(strips, LAT, split_axis=1, concat_axis=0, tiled=True)  19.2 us
    all_to_all x1, blocking collectives, to_rows(): return lax.all_to_all(strips, LAT, split_axis=1, concat_axis=0, tiled=True)  16.5 us
  transfers between devices with their start and end apart: 5, of which 5 were waited for; matrix products, arithmetic and copies ran while one was open for 2% of the time, Pallas kernels for 0%

profile of v1, /device:TPU:1, one launch (start us, length us, event | category | flops | bytes accessed | tf_op | source)
XLA Modules:
  0.0 404.7 jit_solution(9602716292236705308)
XLA Ops:
  2.3 23.9 %scatter_fusion = f32[8,512]{1,0:T(8,128)S(1)} fusion(f32[8,512]{1,0:T(8,128)S(1)} %broadcast.43.clone, s32[512]{0:T(512)S(1)} %reshape.118, f32[512]{0:T(512)S(1)} %reshape.120), kind=kCustom, calls=%fused_computation.2 | custom fusion | flops 512 | bytes 10240 | tf_op jit(solution)/shard_map/scatter-add | solution.py:77
  26.3 15.9 %all_to_all.124 = f32[4,2,8,256]{3,2,1,0:T(8,128)S(1)} all-to-all(f32[4,2,8,256]{3,2,1,0:T(8,128)S(1)} %broadcast_in_dim.20), channel_id=1, replica_groups=mesh['mem'=4,'lat_0'=4,'lat_1'=2,'lat_2'=4,'lat_3'=2] {'mem'}, dimensions={0} | all-to-all | bytes 131072 | tf_op jit(solution)/shard_map/all_to_all | solution.py:34
  42.2 4.6 %fusion.2 = f32[16,8,8,128]{3,1,2,0:T(8,128)S(1)} fusion(f32[16,8,1024,1]{2,1,3,0:T(8,128)S(1)} %bitcast.230, f32[1024,1024]{1,0:T(8,128)} %param.11), kind=kOutput, calls=%fused_computation.8 | convolution fusion | flops 1610612736 | bytes 5242880 | tf_op jit(solution)/shard_map/frn,nbc->fbrc/dot_general | solution.py:70
  46.8 22.3 %all_to_all.125 = f32[128,8,128]{2,1,0:T(8,128)S(1)} all-to-all(f32[128,8,128]{2,1,0:T(8,128)S(1)} %bitcast.231), channel_id=1, replica_groups=mesh['mem'=4,'lat_0'=4,'lat_1'=2,'lat_2'=4,'lat_3'=2] {'lat_0','lat_1','..., dimensions={0} | all-to-all | bytes 1048576 | tf_op jit(solution)/shard_map/all_to_all | solution.py:60
  69.1 1.1 convolution_bitcast_fusion.4
  70.2 1.1 convolution_bitcast_fusion.3
  71.3 1.0 copy.72
  72.3 5.2 %all-to-all-start.2 = ((f32[2,512,128]{2,0,1:T(2,128)}), f32[2,512,128]{2,0,1:T(2,128)S(1)}, u32[]{:S(2)}, u32[]{:S(2)}) async-start(f32[2,512,128]{2,0,1:T(2,128)} %copy.72), calls=%async_computation.2 | async-start | bytes 1048576 | tf_op jit(solution)/shard_map/all_to_all | solution.py:63
  77.5 5.1 %copy.111 = f32[128,8,8,128]{3,2,1,0:T(8,128)} copy(f32[128,8,8,128]{3,1,2,0:T(8,128)} %bitcast.225) | data formatting | bytes 8388608
  82.6 7.2 %all-to-all-done.2 = f32[2,512,128]{2,0,1:T(2,128)S(1)} async-done(((f32[2,512,128]{2,0,1:T(2,128)}), f32[2,512,128]{2,0,1:T(2,128)S(1)}, u32[]{:S(2)}, u32[]{:S(2)}) %all-to-all-start.2) | async-done | bytes 524320 | tf_op jit(solution)/shard_map/all_to_all | solution.py:63
  89.9 6.8 %fusion.25 = f32[2,8,1024]{2,1,0:T(8,128)S(1)} fusion(f32[8,2,8,1024]{3,2,1,0:T(8,128)S(1)} %copy-done.1, f32[8,2,8,8,128]{4,2,3,1,0:T(8,128)S(1)} %bitcast.240, f32[1024,8,128,1,1]{2,1,0,4,3:T(8,128)} %bitcast.226), kind=kOutput, calls=%fused_computation.28 | convolution fusion | flops 1610858496 | bytes 5308416 | tf_op jit(solution)/shard_map/fbrc,nbc->frn/dot_general | solution.py:93
  97.5 3.3 all-to-all-start.3
  100.8 6.8 %all-to-all-done.3 = f32[4,2,8,256]{3,2,1,0:T(8,128)S(1)} async-done(((f32[4,2,8,256]{3,2,1,0:T(8,128)}), f32[4,2,8,256]{3,2,1,0:T(8,128)S(1)}, u32[]{:S(2)}, u32[]{:S(2)}) %all-to-all-start.3) | async-done | bytes 65568 | tf_op jit(solution)/shard_map/all_to_all | solution.py:22
  107.6 3.6 gather_fusion
  111.4 23.9 %scatter_fusion.1 = f32[8,512]{1,0:T(8,128)S(1)} fusion(f32[8,512]{1,0:T(8,128)S(1)} %broadcast.43.clone.1, s32[512]{0:T(512)S(1)} %reshape.118, f32[512]{0:T(512)S(1)} %reshape.126), kind=kCustom, calls=%fused_computation.3 | custom fusion | flops 512 | bytes 10240 | tf_op jit(solution)/shard_map/scatter-add | solution.py:77
  135.3 9.3 %all_to_all.126 = f32[4,2,8,256]{3,2,1,0:T(8,128)S(1)} all-to-all(f32[4,2,8,256]{3,2,1,0:T(8,128)S(1)} %broadcast_in_dim.21), channel_id=1, replica_groups=mesh['mem'=4,'lat_0'=4,'lat_1'=2,'lat_2'=4,'lat_3'=2] {'mem'}, dimensions={0} | all-to-all | bytes 131072 | tf_op jit(solution)/shard_map/all_to_all | solution.py:34
  144.7 5.4 %fusion.1 = f32[16,8,8,128]{3,1,2,0:T(8,128)} fusion(f32[16,8,1024,1]{2,1,3,0:T(8,128)S(1)} %bitcast.232, f32[1024,1024]{1,0:T(8,128)} %param.11), kind=kOutput, calls=%fused_computation.7 | convolution fusion | flops 1610612736 | bytes 5242880 | tf_op jit(solution)/shard_map/frn,nbc->fbrc/dot_general | solution.py:70
  150.1 7.3 %all-to-all-start.5 = ((f32[128,8,128]{2,1,0:T(8,128)}), f32[128,8,128]{2,1,0:T(8,128)S(1)}, u32[]{:S(2)}, u32[]{:S(2)}) async-start(f32[128,8,128]{2,1,0:T(8,128)} %bitcast.46), calls=%async_computation.5 | async-start | bytes 1048576 | tf_op jit(solution)/shard_map/all_to_all | solution.py:60
  158.0 11.8 %all-to-all-done.5 = f32[128,8,128]{2,1,0:T(8,128)S(1)} async-done(((f32[128,8,128]{2,1,0:T(8,128)}), f32[128,8,128]{2,1,0:T(8,128)S(1)}, u32[]{:S(2)}, u32[]{:S(2)}) %all-to-all-start.5) | async-done | bytes 524320 | tf_op jit(solution)/shard_map/all_to_all | solution.py:60
  169.8 1.8 multiply_reduce_fusion.1
  171.7 1.4 dynamic-update-slice
  173.0 1.4 dynamic-update-slice.5
  175.0 7.2 %all-reduce.25 = (f32[4]{0:T(128)S(1)}, f32[4]{0:T(128)S(1)}) all-reduce(f32[4]{0:T(128)S(1)} %dynamic-update-slice, f32[4]{0:T(128)S(1)} %dynamic-update-slice.5), channel_id=1, replica_groups=mesh['mem'=4,'lat_0'=4,'lat_1'=2,'lat_2'=4,'lat_3'=2] {'mem'}, use_global_device_ids=true, to_apply=%add | all-reduce | flops 8 | bytes 64
  183.4 1.4 dynamic-update-slice.6
  184.8 1.4 dynamic-update-slice.1
  186.8 6.7 %all-reduce.23 = (f32[4]{0:T(128)S(1)}, f32[4]{0:T(128)S(1)}) all-reduce(f32[4]{0:T(128)S(1)} %dynamic-update-slice.1, f32[4]{0:T(128)S(1)} %dynamic-update-slice.6), channel_id=1, replica_groups=mesh['mem'=4,'lat_0'=4,'lat_1'=2,'lat_2'=4,'lat_3'=2] {'lat_0'}, use_global_device_ids=true, to_apply=%add.1 | all-reduce | flops 8 | bytes 64
  194.7 1.4 dynamic-update-slice.7
  196.2 1.6 dynamic-update-slice.2
  198.4 3.8 all-reduce.29
  203.3 1.3 dynamic-update-slice.8
  204.7 1.3 dynamic-update-slice.3
  206.6 6.4 %all-reduce.21 = (f32[4]{0:T(128)S(1)}, f32[4]{0:T(128)S(1)}) all-reduce(f32[4]{0:T(128)S(1)} %dynamic-update-slice.3, f32[4]{0:T(128)S(1)} %dynamic-update-slice.8), channel_id=1, replica_groups=mesh['mem'=4,'lat_0'=4,'lat_1'=2,'lat_2'=4,'lat_3'=2] {'lat_2'}, use_global_device_ids=true, to_apply=%add.3 | all-reduce | flops 8 | bytes 64
  214.2 1.3 dynamic-update-slice.9
  215.5 1.3 dynamic-update-slice.4
  216.8 9.8 %all-reduce.27 = (f32[2]{0:T(128)S(1)}, f32[2]{0:T(128)S(1)}) all-reduce(f32[2]{0:T(128)S(1)} %dynamic-update-slice.4, f32[2]{0:T(128)S(1)} %dynamic-update-slice.9), channel_id=1, replica_groups=mesh['mem'=4,'lat_0'=4,'lat_1'=2,'lat_2'=4,'lat_3'=2] {'lat_3'}, use_global_device_ids=true, to_apply=%add.4 | all-reduce | flops 4 | bytes 32
  229.9 1.9 convolution_bitcast_fusion.1
  231.8 1.3 copy.81
  233.0 16.5 %all_to_all.127 = f32[2,512,128]{2,0,1:T(2,128)S(1)} all-to-all(f32[2,512,128]{2,0,1:T(2,128)S(1)} %copy.81), channel_id=1, replica_groups=mesh['mem'=4,'lat_0'=4,'lat_1'=2,'lat_2'=4,'lat_3'=2] {'lat_0','lat_1','..., dimensions={1} | all-to-all | bytes 1048576 | tf_op jit(solution)/shard_map/all_to_all | solution.py:63
  249.7 6.8 %fusion.28 = f32[2,8,1024]{2,1,0:T(8,128)S(1)} fusion(f32[8,2,8,1024]{3,2,1,0:T(8,128)S(1)} %copy-done.1, f32[8,2,8,8,128]{4,2,3,1,0:T(8,128)S(1)} %bitcast.239, f32[1024,8,128,1,1]{2,1,0,4,3:T(8,128)} %bitcast.227), kind=kOutput, calls=%fused_computation.29 | convolution fusion | flops 1610858496 | bytes 5308416 | tf_op jit(solution)/shard_map/fbrc,nbc->frn/dot_general | solution.py:93
  256.6 11.6 %all_to_all.129 = f32[4,2,8,256]{3,2,1,0:T(8,128)S(1)} all-to-all(f32[4,2,8,256]{3,2,1,0:T(8,128)S(1)} %copy.85), channel_id=1, replica_groups=mesh['mem'=4,'lat_0'=4,'lat_1'=2,'lat_2'=4,'lat_3'=2] {'mem'}, dimensions={0} | all-to-all | bytes 131072 | tf_op jit(solution)/shard_map/all_to_all | solution.py:22
  268.2 3.6 gather_fusion.1
  271.9 23.9 %scatter_fusion.2 = f32[8,512]{1,0:T(8,128)S(1)} fusion(f32[8,512]{1,0:T(8,128)S(1)} %broadcast.43, s32[512]{0:T(512)S(1)} %reshape.118, f32[512]{0:T(512)S(1)} %reshape.132), kind=kCustom, calls=%fused_computation.4 | custom fusion | flops 512 | bytes 10240 | tf_op jit(solution)/shard_map/scatter-add | solution.py:77
  295.9 9.3 %all_to_all.128 = f32[4,2,8,256]{3,2,1,0:T(8,128)S(1)} all-to-all(f32[4,2,8,256]{3,2,1,0:T(8,128)S(1)} %broadcast_in_dim.22), channel_id=1, replica_groups=mesh['mem'=4,'lat_0'=4,'lat_1'=2,'lat_2'=4,'lat_3'=2] {'mem'}, dimensions={0} | all-to-all | bytes 131072 | tf_op jit(solution)/shard_map/all_to_all | solution.py:34
  305.2 5.4 %fusion = f32[16,8,8,128]{3,1,2,0:T(8,128)} fusion(f32[16,8,1024,1]{2,1,3,0:T(8,128)S(1)} %bitcast.233, f32[1024,1024]{1,0:T(8,128)} %param.11), kind=kOutput, calls=%fused_computation.6 | convolution fusion | flops 1610612736 | bytes 5242880 | tf_op jit(solution)/shard_map/frn,nbc->fbrc/dot_general | solution.py:70
  310.6 7.2 %all-to-all-start.9 = ((f32[128,8,128]{2,1,0:T(8,128)}), f32[128,8,128]{2,1,0:T(8,128)S(1)}, u32[]{:S(2)}, u32[]{:S(2)}) async-start(f32[128,8,128]{2,1,0:T(8,128)} %bitcast.82), calls=%async_computation.9 | async-start | bytes 1048576 | tf_op jit(solution)/shard_map/all_to_all | solution.py:60
  317.8 1.6 dynamic-update-slice.10
  319.4 10.9 %all-to-all-done.9 = f32[128,8,128]{2,1,0:T(8,128)S(1)} async-done(((f32[128,8,128]{2,1,0:T(8,128)}), f32[128,8,128]{2,1,0:T(8,128)S(1)}, u32[]{:S(2)}, u32[]{:S(2)}) %all-to-all-start.9) | async-done | bytes 524320 | tf_op jit(solution)/shard_map/all_to_all | solution.py:60
  330.3 1.7 fusion.36
  332.0 1.4 dynamic-update-slice.15
  333.4 7.2 %all-reduce.24 = (f32[4]{0:T(128)S(1)}, f32[4]{0:T(128)S(1)}) all-reduce(f32[4]{0:T(128)S(1)} %dynamic-update-slice.10, f32[4]{0:T(128)S(1)} %dynamic-update-slice.15), channel_id=1, replica_groups=mesh['mem'=4,'lat_0'=4,'lat_1'=2,'lat_2'=4,'lat_3'=2] {'mem'}, use_global_device_ids=true, to_apply=%add.10 | all-reduce | flops 8 | bytes 64
  341.2 1.4 dynamic-update-slice.16
  343.2 1.4 dynamic-update-slice.11
  344.5 6.7 %all-reduce.22 = (f32[4]{0:T(128)S(1)}, f32[4]{0:T(128)S(1)}) all-reduce(f32[4]{0:T(128)S(1)} %dynamic-update-slice.11, f32[4]{0:T(128)S(1)} %dynamic-update-slice.16), channel_id=1, replica_groups=mesh['mem'=4,'lat_0'=4,'lat_1'=2,'lat_2'=4,'lat_3'=2] {'lat_0'}, use_global_device_ids=true, to_apply=%add.11 | all-reduce | flops 8 | bytes 64
  351.9 1.4 dynamic-update-slice.17
  353.9 1.4 dynamic-update-slice.12
  355.4 3.8 all-reduce.28
  359.7 1.3 dynamic-update-slice.18
  361.7 1.3 dynamic-update-slice.13
  363.0 6.4 %all-reduce.20 = (f32[4]{0:T(128)S(1)}, f32[4]{0:T(128)S(1)}) all-reduce(f32[4]{0:T(128)S(1)} %dynamic-update-slice.13, f32[4]{0:T(128)S(1)} %dynamic-update-slice.18), channel_id=1, replica_groups=mesh['mem'=4,'lat_0'=4,'lat_1'=2,'lat_2'=4,'lat_3'=2] {'lat_2'}, use_global_device_ids=true, to_apply=%add.13 | all-reduce | flops 8 | bytes 64
  370.0 1.3 dynamic-update-slice.19
  371.9 1.3 dynamic-update-slice.14
  373.2 9.8 %all-reduce.26 = (f32[2]{0:T(128)S(1)}, f32[2]{0:T(128)S(1)}) all-reduce(f32[2]{0:T(128)S(1)} %dynamic-update-slice.14, f32[2]{0:T(128)S(1)} %dynamic-update-slice.19), channel_id=1, replica_groups=mesh['mem'=4,'lat_0'=4,'lat_1'=2,'lat_2'=4,'lat_3'=2] {'lat_3'}, use_global_device_ids=true, to_apply=%add.14 | all-reduce | flops 4 | bytes 32
  386.7 4.4 %all-to-all-start.10 = ((f32[2,512,128]{2,0,1:T(2,128)}), f32[2,512,128]{2,0,1:T(2,128)S(1)}, u32[]{:S(2)}, u32[]{:S(2)}) async-start(f32[2,512,128]{2,0,1:T(2,128)} %copy.90), calls=%async_computation.10 | async-start | bytes 1048576 | tf_op jit(solution)/shard_map/all_to_all | solution.py:63
  391.7 11.9 %all-to-all-done.10 = f32[2,512,128]{2,0,1:T(2,128)S(1)} async-done(((f32[2,512,128]{2,0,1:T(2,128)}), f32[2,512,128]{2,0,1:T(2,128)S(1)}, u32[]{:S(2)}, u32[]{:S(2)}) %all-to-all-start.10) | async-done | bytes 524320 | tf_op jit(solution)/shard_map/all_to_all | solution.py:63
  (103 shorter events, 21.6 us)
Async XLA Ops:
  0.6 68.5 %copy-start = (f32[512,512]{1,0:T(8,128)S(1)}, f32[512,512]{1,0:T(8,128)}, u32[]{:S(2)}) copy-start(f32[512,512]{1,0:T(8,128)} %param.10) | copy-start | bytes 3145732
  2.3 39.8 %copy-start.1 = (f32[8,2,8,1024]{3,2,1,0:T(8,128)S(1)}, f32[8,2,8,1024]{3,2,1,0:T(8,128)}, u32[]{:S(2)}) copy-start(f32[8,2,8,1024]{3,2,1,0:T(8,128)} %param.9) | copy-start | bytes 1572868
  72.3 17.6 %all-to-all-start.2 = ((f32[2,512,128]{2,0,1:T(2,128)}), f32[2,512,128]{2,0,1:T(2,128)S(1)}, u32[]{:S(2)}, u32[]{:S(2)}) async-start(f32[2,512,128]{2,0,1:T(2,128)} %copy.72), calls=%async_computation.2 | async-start | bytes 1048576 | tf_op jit(solution)/shard_map/all_to_all | solution.py:63
  96.8 14.5 %copy-start.2 = (f32[8,64]{1,0:T(8,128)S(1)}, f32[8,64]{1,0:T(8,128)}, u32[]{:S(2)}) copy-start(f32[8,64]{1,0:T(8,128)} %param.13) | copy-start | bytes 6148
  96.8 14.5 %copy-start.3 = (s32[8,64]{1,0:T(8,128)S(1)}, s32[8,64]{1,0:T(8,128)}, u32[]{:S(2)}) copy-start(s32[8,64]{1,0:T(8,128)} %param.14) | copy-start | bytes 6148
  97.5 10.1 %all-to-all-start.3 = ((f32[4,2,8,256]{3,2,1,0:T(8,128)}), f32[4,2,8,256]{3,2,1,0:T(8,128)S(1)}, u32[]{:S(2)}, u32[]{:S(2)}) async-start(f32[4,2,8,256]{3,2,1,0:T(8,128)} %copy.76), calls=%async_computation.3 | async-start | bytes 131072 | tf_op jit(solution)/shard_map/all_to_all | solution.py:22
  135.3 22.1 %copy-start.8 = (u32[256]{0:T(256)S(1)}, u32[256]{0:T(256)}, u32[]{:S(2)}) copy-start(u32[256]{0:T(256)} %constant.138) | copy-start | bytes 3076
  144.6 29.7 %copy-start.7 = (u32[256]{0:T(256)S(1)}, u32[256]{0:T(256)}, u32[]{:S(2)}) copy-start(u32[256]{0:T(256)} %constant.143) | copy-start | bytes 3076
  144.7 41.5 %copy-start.6 = (u32[256]{0:T(256)S(1)}, u32[256]{0:T(256)}, u32[]{:S(2)}) copy-start(u32[256]{0:T(256)} %constant.148) | copy-start | bytes 3076
  144.7 53.1 %copy-start.5 = (u32[256]{0:T(256)S(1)}, u32[256]{0:T(256)}, u32[]{:S(2)}) copy-start(u32[256]{0:T(256)} %constant.153) | copy-start | bytes 3076
  144.7 61.3 %copy-start.4 = (u32[256]{0:T(256)S(1)}, u32[256]{0:T(256)}, u32[]{:S(2)}) copy-start(u32[256]{0:T(256)} %constant.158) | copy-start | bytes 3076
  150.1 19.7 %all-to-all-start.5 = ((f32[128,8,128]{2,1,0:T(8,128)}), f32[128,8,128]{2,1,0:T(8,128)S(1)}, u32[]{:S(2)}, u32[]{:S(2)}) async-start(f32[128,8,128]{2,1,0:T(8,128)} %bitcast.46), calls=%async_computation.5 | async-start | bytes 1048576 | tf_op jit(solution)/shard_map/all_to_all | solution.py:60
  310.6 19.7 %all-to-all-start.9 = ((f32[128,8,128]{2,1,0:T(8,128)}), f32[128,8,128]{2,1,0:T(8,128)S(1)}, u32[]{:S(2)}, u32[]{:S(2)}) async-start(f32[128,8,128]{2,1,0:T(8,128)} %bitcast.82), calls=%async_computation.9 | async-start | bytes 1048576 | tf_op jit(solution)/shard_map/all_to_all | solution.py:60
  386.7 17.0 %all-to-all-start.10 = ((f32[2,512,128]{2,0,1:T(2,128)}), f32[2,512,128]{2,0,1:T(2,128)S(1)}, u32[]{:S(2)}, u32[]{:S(2)}) async-start(f32[2,512,128]{2,0,1:T(2,128)} %copy.90), calls=%async_computation.10 | async-start | bytes 1048576 | tf_op jit(solution)/shard_map/all_to_all | solution.py:63
